TPU v7x, 256 devices: a whole 4x4x8 slice. The times are simulated.
256 devices in a mesh: sub: 8 (over y, core), dev: 32 (over z, x).
Axes of the slice: x: 4, y: 4, z: 8, core: 2. Of those that a mesh axis runs over, the one named last changes fastest.
Arguments:
- load: float32 [262144, 256], P(('sub', 'dev')), may hold values from -6 to 6
- schur: bfloat16 [262144, 1024], P(('sub', 'dev')), as said below
- local_inverse: bfloat16 [262144, 1024], P(('sub', 'dev')), as said below
- coarse_basis: float32 [4096, 1024], P(('sub', 'dev')), may hold values from -0.1875 to 0.1875
- coarse_inverse: float32 [1024, 1024], P('dev'), as said below
- dof_lists: int32 [256, 4, 256], P(('sub', 'dev')), may hold values from -1 to 1023, as said below
- coarse_map: int32 [256, 16], P(('sub', 'dev')), may hold values from 0 to 1023, as said below
- stiffness: float32 [256], replicated, may hold values from 1 to 1000
Outputs:
- solution: float32 [262144, 256], P(('sub', 'dev'))
- residual: float32 [262144, 256], P(('sub', 'dev'))
Inputs may be any that keep to these rules, and one draw needn't show every extreme that they name: dof_lists[p, k, j] for j below that pair's count names the local unknown of subdomain p that is the j-th one shared with its neighbour in direction k, and -1 past the count; the entry of the neighbour in the opposite direction at the same j names the same unknown. The named entries of a subdomain are exactly 0 to its count minus one, each once; directions without a neighbour are all -1; one pair shares 256 unknowns and one subdomain has 1024. `coarse_map`: distinct within a subdomain; every coarse unknown is named by exactly four primal unknowns in all. `schur`: each block is symmetric positive definite. `local_inverse`: each block is symmetric positive definite. `coarse_inverse`: symmetric positive definite.
All inputs are finite; a program needn't handle non-finite values.
Results may differ from a plain program's by a relative error of at most 0.0093.
Values sent between devices are 32-bit elements; how exact they have to be, the bound alone decides.
No kernel may reach another device: no remote copies, remote signals or barrier semaphores. Data moves between devices by JAX's collectives and lax.ppermute only.
A program may use at most 64 MiB of HBM per device.

v0:
```python
import jax
import jax.numpy as jnp
from jax import lax
from jax.sharding import PartitionSpec as P

ITERS = 2


def with_halo(array, sides, width):
    for axis, dim in sides:
        count, length = (lax.axis_size(axis), array.shape[dim])
        up = [(i, (i + 1) % count) for i in range(count - 1)]
        down = [(j, i) for i, j in up]
        last = lax.slice_in_dim(array, length - width, length, axis=dim)
        first = lax.slice_in_dim(array, 0, width, axis=dim)
        before = lax.ppermute(last, axis, up)
        after = lax.ppermute(first, axis, down)
        array = jnp.concatenate([before, array, after], axis=dim)
    return array


def shards(
    load, schur, local_inverse, coarse_basis, coarse_inverse, dof_lists, coarse_map, stiffness
):
    largest_value = lax.Precision.HIGHEST
    unknowns = schur.shape[0]
    coarse_size = coarse_inverse.shape[1]
    dof_rows = dof_lists[0]
    in_use = dof_rows >= 0
    live_count = jnp.sum(in_use.astype(jnp.int32))
    active_mask = (jnp.arange(unknowns, dtype=jnp.int32) < live_count).astype(jnp.float32)[:, None]
    dev_size = lax.axis_size("dev")
    myself = lax.axis_index("sub") * dev_size + lax.axis_index("dev")
    shifts = jnp.array([-dev_size, dev_size, -1, 1], dtype=jnp.int32)
    neighbours = jnp.clip(myself + shifts, 0, stiffness.shape[0] - 1)
    own_coefficient = stiffness[myself]
    slot_weight = own_coefficient / (own_coefficient + stiffness[neighbours])
    target = jnp.where(in_use, dof_rows, unknowns)
    safe_rows = jnp.where(in_use, dof_rows, 0)
    weights = (
        jnp.zeros((unknowns + 1,), jnp.float32)
        .at[target]
        .set(jnp.broadcast_to(slot_weight[:, None], dof_rows.shape))[:unknowns][:, None]
    )
    in_use_float = in_use.astype(jnp.float32)[..., None]
    selector = (jnp.arange(coarse_size, dtype=jnp.int32)[:, None] == coarse_map[0][None, :]).astype(
        jnp.float32
    )

    def assemble(values):
        packed = values[safe_rows] * in_use_float
        from_sub = with_halo(packed[0:2], (("sub", 0),), 1)
        from_dev = with_halo(packed[2:4], (("dev", 0),), 1)
        incoming = jnp.stack([from_sub[0], from_sub[3], from_dev[0], from_dev[3]], axis=0)
        padded = jnp.concatenate([values, jnp.zeros((1, values.shape[1]), jnp.float32)], axis=0)
        return padded.at[target.reshape(-1)].add(incoming.reshape(-1, values.shape[1]))[:unknowns]

    def block_product(matrix, vectors):
        narrow = vectors.astype(jnp.bfloat16)
        result = jnp.dot(matrix, narrow, preferred_element_type=jnp.float32)
        return active_mask * result

    def coarse_term(weighted_vector):
        projected_vector = jnp.dot(coarse_basis, weighted_vector, precision=largest_value)
        return jnp.dot(selector, projected_vector, precision=largest_value)

    def coarse_sum(weighted_vector):
        return lax.psum(coarse_term(weighted_vector), ("sub", "dev"))

    def global_dot(left, right):
        return lax.psum(jnp.sum(weights * left * right, axis=0), ("sub", "dev"))

    def precondition(residual, coarse_rhs):
        weighted_vector = weights * residual
        local_part = block_product(local_inverse, weighted_vector)
        solved_rows = jnp.dot(coarse_inverse, coarse_rhs, precision=largest_value)
        solved = lax.all_gather(solved_rows, "dev", axis=0, tiled=True)
        selected_entries = lax.dot_general(
            selector, solved, (((0,), (0,)), ((), ())), precision=largest_value
        )
        spread_back = lax.dot_general(
            coarse_basis, selected_entries, (((0,), (0,)), ((), ())), precision=largest_value
        )
        return assemble(weights * (local_part + active_mask * spread_back))

    residual = assemble(active_mask * load)
    coarse_rhs = coarse_sum(weights * residual)
    precond = precondition(residual, coarse_rhs)
    norm_now = global_dot(residual, precond)
    direction = precond
    solution = jnp.zeros_like(residual)
    for iteration in range(ITERS):
        applied = assemble(block_product(schur, direction))
        more_left = iteration + 1 < ITERS
        curvature = global_dot(direction, applied)
        step_size = norm_now / curvature
        solution = solution + step_size * direction
        residual = residual - step_size * applied
        if more_left:
            coarse_rhs = coarse_sum(weights * residual)
            precond = precondition(residual, coarse_rhs)
            norm_next = global_dot(residual, precond)
            direction = precond + norm_next / norm_now * direction
            norm_now = norm_next
    return (solution, residual)


def solution(mesh):
    placed = (
        P(("sub", "dev"), None),
        P(("sub", "dev"), None),
        P(("sub", "dev"), None),
        P(("sub", "dev"), None),
        P("dev", None),
        P(("sub", "dev"), None, None),
        P(("sub", "dev"), None),
        P(),
    )
    return jax.shard_map(
        shards,
        mesh=mesh,
        in_specs=placed,
        out_specs=(P(("sub", "dev"), None), P(("sub", "dev"), None)),
        check_vma=False,
    )
```

profile of v0, /device:TPU:1, one launch (start us, length us, event | category | flops | bytes accessed | tf_op | source)
XLA Modules:
  0.0 1136.1 jit_solution(10563207238050007719)
XLA Ops:
  11.5 4.7 gather_fusion.1
  18.6 4.6 collective-permute-start
  24.5 4.7 collective-permute-start.2
  29.2 3.1 collective-permute-start.1
  35.8 4.3 scatter_custom_fusion
  40.2 2.3 pad_maximum_fusion
  42.5 8.0 scatter_fusion
  52.8 257.3 %all-reduce.9.cloned.1.call-done = f32[1024,256]{1,0:T(8,128)} async-done(((f32[1024,256]{1,0:T(8,128)}), f32[1024,256]{1,0:T(8,128)}) %all-reduce.9.cloned.1.call-update) | async-done | bytes 1048592 | tf_op jit(solution)/shard_map/psum | solution.py:68
  310.1 2.5 convolution_bitcast_fusion.1
  312.7 2.0 fusion.12
  314.6 70.9 %all-gather.3.cloned.1.call-done = f32[1024,256]{1,0:T(8,128)} async-done(((f32[32,256]{1,0:T(8,128)}), f32[1024,256]{1,0:T(8,128)}) %all-gather.3.cloned.1.call-update) | async-done | bytes 1048592 | tf_op jit(solution)/shard_map/all_gather | solution.py:77
  387.4 2.1 fusion.3
  389.5 2.5 copy.40
  392.0 5.9 gather_fusion.2
  399.5 8.2 collective-permute-start.4
  408.9 4.0 collective-permute-start.6
  413.0 2.1 collective-permute-start.5
  418.1 2.6 collective-permute-done.5
  421.7 9.8 scatter_fusion.1
  431.5 3.6 fusion.7
  435.2 2.5 copy.41
  437.7 5.9 gather_fusion.3
  445.1 2.1 collective-permute-start.8
  448.5 4.0 collective-permute-start.10
  452.5 3.0 collective-permute-start.9
  457.3 3.1 collective-permute-done.9
  461.5 9.8 scatter_fusion.2
  473.2 81.0 %all-reduce.5 = (f32[256]{0:T(256)S(1)}, f32[256]{0:T(256)S(1)}) all-reduce(f32[256]{0:T(256)S(1)} %get-tuple-element.5, f32[256]{0:T(256)S(1)} %get-tuple-element.4), channel_id=1, replica_groups=mesh['sub'=8,'dev'=32] {'sub','dev'}, use_global_device_ids=true, to_apply=%region_6.7 | all-reduce | flops 512 | bytes 4096 | tf_op jit(solution)/shard_map/psum | solution.py:71
  559.1 250.3 %all-reduce.11.cloned.1.call-done = f32[1024,256]{1,0:T(8,128)} async-done(((f32[1024,256]{1,0:T(8,128)}), f32[1024,256]{1,0:T(8,128)}) %all-reduce.11.cloned.1.call-update) | async-done | bytes 1048592 | tf_op jit(solution)/shard_map/psum | solution.py:68
  809.4 2.5 convolution_bitcast_fusion
  811.9 2.0 fusion.14
  813.9 70.1 %all-gather.5.cloned.1.call-done = f32[1024,256]{1,0:T(8,128)} async-done(((f32[32,256]{1,0:T(8,128)}), f32[1024,256]{1,0:T(8,128)}) %all-gather.5.cloned.1.call-update) | async-done | bytes 1048592 | tf_op jit(solution)/shard_map/all_gather | solution.py:77
  885.8 2.1 fusion.5
  889.4 4.7 gather_fusion.4
  895.6 8.0 collective-permute-start.12
  905.0 4.0 collective-permute-start.14
  914.1 2.6 collective-permute-done.13
  916.7 9.4 scatter_fusion.3
  928.0 77.8 %psum.46 = f32[256]{0:T(256)S(1)} all-reduce(f32[256]{0:T(256)S(1)} %multiply_reduce_fusion.1), channel_id=1, replica_groups=mesh['sub'=8,'dev'=32] {'sub','dev'}, use_global_device_ids=true, to_apply=%region_13.14 | all-reduce | flops 256 | bytes 2048 | tf_op jit(solution)/shard_map/psum | solution.py:71
  1010.0 2.5 copy.43
  1012.5 5.9 gather_fusion.5
  1019.9 2.8 collective-permute-start.16
  1024.1 4.0 collective-permute-start.18
  1028.1 2.5 collective-permute-start.17
  1033.8 2.0 collective-permute-done.17
  1036.8 9.8 scatter_fusion.4
  1048.4 77.7 %psum.47 = f32[256]{0:T(256)S(1)} all-reduce(f32[256]{0:T(256)S(1)} %multiply_reduce_fusion), channel_id=1, replica_groups=mesh['sub'=8,'dev'=32] {'sub','dev'}, use_global_device_ids=true, to_apply=%region_16.17 | all-reduce | flops 256 | bytes 2048 | tf_op jit(solution)/shard_map/psum | solution.py:71
  1126.1 3.4 multiply_subtract_fusion
  (119 shorter events, 61.2 us)
Async XLA Ops:
  7.2 305.5 %copy-start = (bf16[1024,1024]{1,0:T(8,128)(2,1)S(1)}, bf16[1024,1024]{1,0:T(8,128)(2,1)}, u32[]{:S(2)}) copy-start(bf16[1024,1024]{1,0:T(8,128)(2,1)} %param.11) | copy-start | bytes 6291460
  7.2 302.9 %all-reduce.9.cloned.1.call-start = ((), (), s32[]{:S(2)}) async-start(), calls=%async_computation | async-start | bytes 2097152 | tf_op jit(solution)/shard_map/psum | solution.py:68
  11.5 4.7 copy-start.3
  17.6 14.7 %copy-start.17 = (s32[4]{0:T(128)S(1)}, s32[4]{0:T(128)}, u32[]{:S(2)}) copy-start(s32[4]{0:T(128)} %constant.6.clone) | copy-start | bytes 52
  17.6 14.8 %copy-start.1 = (f32[256]{0:T(256)S(1)}, f32[256]{0:T(256)}, u32[]{:S(2)}) copy-start(f32[256]{0:T(256)} %param.16) | copy-start | bytes 3076
  17.6 16.8 %copy-start.15 = (s32[1,4,256]{2,1,0:T(4,128)S(1)}, s32[1,4,256]{2,1,0:T(4,128)}, u32[]{:S(2)}) copy-start(s32[1,4,256]{2,1,0:T(4,128)} %param.14) | copy-start | bytes 12292
  18.6 21.5 %collective-permute-start = (f32[1,256,256]{2,1,0:T(8,128)}, f32[1,256,256]{2,1,0:T(8,128)}, u32[]{:S(2)}, u32[]{:S(2)}) collective-permute-start(f32[1,256,256]{2,1,0:T(8,128)} %get-tuple-element.26), channel_id=1, source_target_pairs={{0,32},{32,64},{64,96},{96,128},{128,160},{160,192},{192,224},{1,3... | collective-permute-start | bytes 786440 | tf_op jit(solution)/shard_map/ppermute | solution.py:16
  23.2 16.9 %collective-permute-start.3 = (f32[1,256,256]{2,1,0:T(8,128)}, f32[1,256,256]{2,1,0:T(8,128)}, u32[]{:S(2)}, u32[]{:S(2)}) collective-permute-start(f32[1,256,256]{2,1,0:T(8,128)} %get-tuple-element.27), channel_id=1, source_target_pairs={{1,0},{2,1},{3,2},{4,3},{5,4},{6,5},{7,6},{8,7},{9,8},{10,9},{11,1... | collective-permute-start | bytes 786440 | tf_op jit(solution)/shard_map/ppermute | solution.py:17
  24.5 15.6 %collective-permute-start.2 = (f32[1,256,256]{2,1,0:T(8,128)}, f32[1,256,256]{2,1,0:T(8,128)}, u32[]{:S(2)}, u32[]{:S(2)}) collective-permute-start(f32[1,256,256]{2,1,0:T(8,128)} %get-tuple-element.28), channel_id=1, source_target_pairs={{0,1},{1,2},{2,3},{3,4},{4,5},{5,6},{6,7},{7,8},{8,9},{9,10},{10,1... | collective-permute-start | bytes 786440 | tf_op jit(solution)/shard_map/ppermute | solution.py:16
  29.2 10.9 collective-permute-start.1
  42.4 8.0 copy-start.13
  50.5 0.7 copy-start.16
  51.2 258.9 %copy-start.14 = (f32[32,1024]{1,0:T(8,128)S(1)}, f32[32,1024]{1,0:T(8,128)}, u32[]{:S(2)}) copy-start(f32[32,1024]{1,0:T(8,128)} %param.13) | copy-start | bytes 393220
  52.8 332.8 %all-gather.3.cloned.1.call-start = ((), (), s32[]{:S(2)}) async-start(), calls=%async_computation.1 | async-start | bytes 1081344 | tf_op jit(solution)/shard_map/all_gather | solution.py:77
  312.6 496.8 %all-reduce.11.cloned.1.call-start = ((), (), s32[]{:S(2)}) async-start(), calls=%async_computation.2 | async-start | bytes 2097152 | tf_op jit(solution)/shard_map/psum | solution.py:68
  385.5 1.9 copy-start.11
  399.4 15.7 %copy-start.5 = (f32[1024,256]{1,0:T(8,128)S(1)}, f32[1024,256]{1,0:T(8,128)}, u32[]{:S(2)}) copy-start(f32[1024,256]{1,0:T(8,128)} %copy.40) | copy-start | bytes 3145732
  399.5 16.7 %collective-permute-start.4 = (f32[1,256,256]{2,1,0:T(8,128)S(1)}, f32[1,256,256]{2,1,0:T(8,128)S(1)}, u32[]{:S(2)}, u32[]{:S(2)}) collective-permute-start(f32[1,256,256]{2,1,0:T(8,128)S(1)} %get-tuple-element.22), channel_id=1, source_target_pairs={{0,32},{32,64},{64,96},{96,128},{128,160},{160,192},{192,224},{1,3... | collective-permute-start | bytes 786440 | tf_op jit(solution)/shard_map/ppermute | solution.py:16
  407.6 8.7 collective-permute-start.7
  408.9 9.1 collective-permute-start.6
  413.0 7.7 collective-permute-start.5
  445.0 10.5 copy-start.6
  445.1 11.4 %collective-permute-start.8 = (f32[1,256,256]{2,1,0:T(8,128)S(1)}, f32[1,256,256]{2,1,0:T(8,128)S(1)}, u32[]{:S(2)}, u32[]{:S(2)}) collective-permute-start(f32[1,256,256]{2,1,0:T(8,128)S(1)} %get-tuple-element.18), channel_id=1, source_target_pairs={{0,32},{32,64},{64,96},{96,128},{128,160},{160,192},{192,224},{1,3... | collective-permute-start | bytes 786440 | tf_op jit(solution)/shard_map/ppermute | solution.py:16
  447.2 9.4 collective-permute-start.11
  448.5 8.8 collective-permute-start.10
  452.5 8.0 collective-permute-start.9
  555.5 1.0 copy-start.7
  558.8 253.1 %copy-start.8 = (f32[1024,256]{1,0:T(8,128)S(1)}, f32[1024,256]{1,0:T(8,128)}, u32[]{:S(2)}) copy-start(f32[1024,256]{1,0:T(8,128)} %copy-done.7) | copy-start | bytes 3145732
  558.8 325.2 %all-gather.5.cloned.1.call-start = ((), (), s32[]{:S(2)}) async-start(), calls=%async_computation.3 | async-start | bytes 1081344 | tf_op jit(solution)/shard_map/all_gather | solution.py:77
  813.9 71.9 %copy-start.12 = (f32[256,1024]{1,0:T(8,128)S(1)}, f32[256,1024]{1,0:T(8,128)}, u32[]{:S(2)}) copy-start(f32[256,1024]{1,0:T(8,128)} %fusion.14) | copy-start | bytes 3145732
  895.6 16.3 %collective-permute-start.12 = (f32[1,256,256]{2,1,0:T(8,128)S(1)}, f32[1,256,256]{2,1,0:T(8,128)S(1)}, u32[]{:S(2)}, u32[]{:S(2)}) collective-permute-start(f32[1,256,256]{2,1,0:T(8,128)S(1)} %get-tuple-element.14), channel_id=1, source_target_pairs={{0,32},{32,64},{64,96},{96,128},{128,160},{160,192},{192,224},{1,3... | collective-permute-start | bytes 786440 | tf_op jit(solution)/shard_map/ppermute | solution.py:16
  903.7 8.7 collective-permute-start.15
  905.0 9.1 collective-permute-start.14
  909.0 7.7 collective-permute-start.13
  926.1 79.6 %copy-start.2 = (f32[1025,256]{1,0:T(8,128)S(1)}, f32[1025,256]{1,0:T(8,128)}, u32[]{:S(2)}) copy-start(f32[1025,256]{1,0:T(8,128)} %scatter_fusion.1) | copy-start | bytes 3148804
  1005.7 2.5 copy-start.10
  1007.2 1.0 copy-start.9
  1019.8 10.7 copy-start.4
  1019.9 11.7 %collective-permute-start.16 = (f32[1,256,256]{2,1,0:T(8,128)S(1)}, f32[1,256,256]{2,1,0:T(8,128)S(1)}, u32[]{:S(2)}, u32[]{:S(2)}) collective-permute-start(f32[1,256,256]{2,1,0:T(8,128)S(1)} %get-tuple-element.10), channel_id=1, source_target_pairs={{0,32},{32,64},{64,96},{96,128},{128,160},{160,192},{192,224},{1,3... | collective-permute-start | bytes 786440 | tf_op jit(solution)/shard_map/ppermute | solution.py:16
  1022.8 10.0 collective-permute-start.19
  1024.1 9.7 collective-permute-start.18
  1028.1 7.7 collective-permute-start.17
Sparse Core Ops, SparseCore 0:
  52.9 257.1 all-reduce.8
  313.6 71.9 all-gather.2
  558.9 250.4 all-reduce.10
  812.0 71.9 all-gather.4
where the time goes:
time: 1140 us
  waiting for transfers between devices  666 us (58%)
  blocking collectives  236 us (21%)
  other arithmetic  76.2 us (7%)
  starting transfers between devices  65.8 us (6%)
  local copies, waits for them, and re-layouts  50.8 us (4%)
  matrix products  26.6 us (2%)
  between operations  14.4 us (1%)
    psum x2, waiting for transfers between devices, coarse_sum(): return lax.psum(coarse_term(weighted_vector), ('sub', 'dev'))  508 us
    psum x3, blocking collectives, global_dot(): return lax.psum(jnp.sum(weights * left * right, axis=0), ('sub', 'dev'))  236 us
    all_gather x2, waiting for transfers between devices, precondition(): solved = lax.all_gather(solved_rows, 'dev', axis=0, tiled=True)  141 us
    scatter-add x5, other arithmetic, assemble(): padded.at[target.reshape(-1)].add(incoming.reshape(-1, values.shape[1]))  46.9 us
    ppermute x10, starting transfers between devices, with_halo(): before = lax.ppermute(last, axis, up)  46.4 us
    gather x5, local copies, waits for them, and re-layouts, assemble(): packed = values[safe_rows] * in_use_float  27.1 us
  transfers between devices with their start and end apart: 24, of which 15 were waited for; matrix products, arithmetic and copies ran while one was open for 1% of the time, Pallas kernels for 0%

commit v1 on v0

v1 whole, which is shorter than its diff:
```python
import jax
import jax.numpy as jnp
import numpy as np
from jax import lax
from jax.experimental import pallas as pl
from jax.experimental.pallas import tpu as pltpu
from jax.sharding import PartitionSpec as P

F32, BF16 = jnp.float32, jnp.bfloat16
EXACT = lax.Precision.HIGHEST
NI, NRHS, NCL, CAP, NC = 1024, 256, 16, 256, 1024
N_SUB, N_DEV, N_X, N_Z = 8, 32, 4, 8
PEERS = N_SUB * N_X
MIB = 1 << 20
NN = (((1,), (0,)), ((), ()))
NT = (((1,), (1,)), ((), ()))


def mm(a, b, dims=NN, precision=None):
    return lax.dot_general(a, b, dims, precision=precision, preferred_element_type=F32)


def pieces(v, count):
    out = []
    for i in range(count):
        part = v.astype(BF16)
        out.append(part)
        if i + 1 < count:
            v = v - part.astype(F32)
    return out


def shape(*dims, dtype=F32):
    return jax.ShapeDtypeStruct(dims, dtype)


def run(body, outs, ins, smem=(), scratch=(), limit=40, flops=0):
    vmem = pl.BlockSpec(memory_space=pltpu.VMEM)
    specs = [pl.BlockSpec(memory_space=pltpu.SMEM) if i in smem else vmem for i in range(len(ins))]
    size = sum(int(np.prod(a.shape)) * a.dtype.itemsize for a in list(ins) + list(outs))
    return pl.pallas_call(
        body,
        out_shape=list(outs),
        in_specs=specs,
        out_specs=[vmem] * len(outs),
        scratch_shapes=list(scratch),
        compiler_params=pltpu.CompilerParams(vmem_limit_bytes=limit * MIB),
        cost_estimate=pl.CostEstimate(flops=flops, bytes_accessed=size, transcendentals=0),
        name=body.__name__,
    )(*ins)


def slot_weights(me, stiffness):
    s, d = me[0], me[1]
    p = s * N_DEV + d
    own = jnp.full((1, NRHS), stiffness[p], F32)
    out = []
    for shift in (-N_DEV, N_DEV, -1, 1):
        q = jnp.clip(p + shift, 0, N_SUB * N_DEV - 1)
        out.append(own / (own + jnp.full((1, NRHS), stiffness[q], F32)))
    return out


def iota(dims, axis):
    return lax.broadcasted_iota(jnp.int32, dims, axis)


def slot_major(dof):
    wide = jnp.concatenate([dof.astype(F32), jnp.zeros((4, CAP), F32)], axis=0)
    columns = jnp.transpose(wide)
    lanes = iota((CAP, NI), 1).astype(F32)
    return [jnp.where(columns[:, k : k + 1] == lanes, 1.0, 0.0).astype(BF16) for k in range(4)]


def unknown_major(dof):
    rows = iota((NI, CAP), 0)
    return [jnp.where(rows == dof[k : k + 1, :], 1.0, 0.0).astype(BF16) for k in range(4)]


def rows_of(k):
    return slice(k * CAP, (k + 1) * CAP)


HROWS = CAP + NCL + 8


def prepare(me, stiffness, dof, load, basis, names, h0, h1, h2, h3, wide, perm):
    for k, block in enumerate(slot_major(dof[...])):
        perm[rows_of(k), :] = block
    for i, part in enumerate(pieces(load[...], 3)):
        wide[:, i * NRHS : (i + 1) * NRHS] = part
    basis_parts = jnp.concatenate(pieces(basis[...], 3), axis=0)
    weights = slot_weights(me, stiffness)
    for k, h in enumerate((h0, h1, h2, h3)):
        both = mm(perm[rows_of(k), :], wide[...])
        h[0:CAP, :] = both[:, :NRHS] + both[:, NRHS : 2 * NRHS] + both[:, 2 * NRHS :]
        three = mm(basis_parts, perm[rows_of(k), :], NT)
        h[CAP : CAP + NCL, :] = weights[k] * (
            three[:NCL] + three[NCL : 2 * NCL] + three[2 * NCL :]
        )
        h[CAP + NCL :, :] = jnp.concatenate([names[...], names[...]], axis=1)


def permute_blocks(dof, schur, inverse, schur_out, inverse_out, perm, perm_t, half):
    for k, block in enumerate(slot_major(dof[...])):
        perm[rows_of(k), :] = block
    for k, block in enumerate(unknown_major(dof[...])):
        perm_t[:, rows_of(k)] = block
    for source, target in ((inverse, inverse_out), (schur, schur_out)):
        for k in range(4):
            half[rows_of(k), :] = mm(perm[rows_of(k), :], source[...]).astype(BF16)
        for k in range(4):
            target[rows_of(k), :] = mm(half[rows_of(k), :], perm_t[...]).astype(BF16)


def block_product(matrix, wide, k):
    both = mm(matrix[rows_of(k), :], wide[...])
    return both[:, :NRHS] + both[:, NRHS:]


def split_into(wide, k, v):
    for i, part in enumerate(pieces(v, 2)):
        wide[rows_of(k), i * NRHS : (i + 1) * NRHS] = part


def lane_slot(j):
    return lax.div(iota((8, 128), 1), NCL) == j


def begin(
    me, stiffness, inverse, h0, h1, h2, h3, g0, g1, g2, g3,
    send, rows_out, columns_out, r_out, e0, e1, e2, e3, wide,
):
    hs, gs, es = (h0, h1, h2, h3), (g0, g1, g2, g3), (e0, e1, e2, e3)
    s, d = me[0], me[1]
    x = lax.rem(d, N_X)
    odd = lax.rem(s, 2)
    own = odd * 4 + x
    across, over, edge = (
        (1 - odd) * 4 + x,
        (1 - odd) * 4 + lax.rem(x + 1, 4),
        (1 - odd) * 4 + lax.rem(x + 2, 4),
    )
    places = (
        jnp.where(odd == 1, across, over),
        jnp.where(odd == 1, over, across),
        jnp.where(x > 0, odd * 4 + x - 1, edge),
        jnp.where(x < N_X - 1, odd * 4 + x + 1, edge),
    )
    weights = slot_weights(me, stiffness)
    rows_out[...] = jnp.zeros_like(rows_out)
    total = jnp.zeros((128, NRHS), F32)
    for k in range(4):
        rows_out[pl.ds(pl.multiple_of(own * NCL, NCL), NCL), rows_of(k)] = hs[k][CAP : CAP + NCL, :]
        rows_out[pl.ds(pl.multiple_of(places[k] * NCL, NCL), NCL), rows_of(k)] = gs[k][
            CAP : CAP + NCL, :
        ]
        total = total + mm(rows_out[:, rows_of(k)], hs[k][0:CAP, :], precision=EXACT)
    columns_out[...] = jnp.transpose(rows_out[...])
    flipped = jnp.transpose(total)
    zero = jnp.zeros((8, 128), F32)
    line = iota((8, 128), 0)
    mine = jnp.where(lane_slot(own), hs[0][CAP + NCL :, 0:128], zero)
    before = jnp.where(lane_slot(s) & (x == 0), gs[2][CAP + NCL :, 0:128], zero)
    after = jnp.where(lane_slot(s) & (x == N_X - 1), gs[3][CAP + NCL :, 0:128], zero)
    extra = jnp.where(line == 0, mine, jnp.where(line == 1, before, jnp.where(line == 2, after, zero)))
    for m in range(PEERS):
        send[m * 16 : m * 16 + 8, :] = flipped[m * 8 : m * 8 + 8, :]
        send[m * 16 + 8 : m * 16 + 16, :] = extra
    for k in range(4):
        r = hs[k][0:CAP, :] + gs[k][0:CAP, :]
        r_out[rows_of(k), :] = r
        split_into(wide, k, weights[k] * r)
    for k in range(4):
        es[k][...] = weights[k] * block_product(inverse, wide, k)


def layout(m):
    s, x = divmod(m, N_X)
    odd = s % 2
    keep = [odd * 4 + x, (1 - odd) * 4 + x]
    keep += [odd * 4 + v for v in (x - 1, x + 1) if 0 <= v < N_X]
    moves = []
    other = s + 1 if odd else s - 1
    if 0 <= other < N_SUB:
        moves.append(((1 - odd) * 4 + (x + 1) % 4, other // 2, (1 - odd) * 4 + x))
    if x in (0, N_X - 1):
        moves.append(((1 - odd) * 4 + (x + 2) % 4, 4 if x == 0 else 5, s))
    return s // 2, keep, moves


def lanes_in(slots):
    at = lax.div(iota((8, 128), 1), NCL)
    hit = at == slots[0]
    for j in slots[1:]:
        hit = hit | (at == j)
    return hit


def roll_slots(v, shift):
    shift = (shift * NCL) % 128
    return pltpu.roll(v, shift, 1) if shift else v


def spread(tiles):
    groups = [jnp.zeros((8, 128), F32) for _ in range(6)]
    for m in range(PEERS):
        base, keep, moves = layout(m)
        tile = tiles(m)
        groups[base] = groups[base] + jnp.where(lanes_in(keep), tile, 0.0)
        for here, group, there in moves:
            part = roll_slots(jnp.where(lanes_in([here]), tile, 0.0), there - here)
            groups[group] = groups[group] + part
    return jnp.concatenate(groups, axis=1)


def fold(groups, pick, out):
    three = mm(jnp.concatenate(pieces(groups, 3), axis=0), pick, NT)
    result = three[0:8] + three[8:16] + three[16:24]
    for z in range(N_Z):
        out[z * 8 : z * 8 + 8, :] = result


def gather_first(received, out, pick_out):
    groups = spread(lambda m: received[m * 16 : m * 16 + 8, :])
    ids = [jnp.zeros((8, 128), F32) for _ in range(6)]
    for m in range(PEERS):
        extra = received[m * 16 + 8 : m * 16 + 16, :]
        base = m // 8
        ids[base] = ids[base] + extra
        ids[4] = ids[4] + extra
        ids[5] = ids[5] + extra
    index = jnp.concatenate(
        [ids[0][0:1], ids[1][0:1], ids[2][0:1], ids[3][0:1], ids[4][1:2], ids[5][2:3]], axis=1
    ).astype(jnp.int32)
    pick = jnp.where(iota((NC, 768), 0) == index, 1.0, 0.0).astype(BF16)
    pick_out[...] = pick
    fold(groups, pick, out)


def gather_again(received, pick, out):
    fold(spread(lambda m: received[m * 8 : m * 8 + 8, :]), pick[...], out)


def coarse_solve(me, received, k0, k1, k2, k3, out, rows):
    x = lax.rem(me[1], N_X)
    for i, block in enumerate((k0, k1, k2, k3)):
        at = lax.rem(x + (N_X - i), N_X) * 32
        rows[pl.ds(pl.multiple_of(at, 32), 32), :] = block[...]
    rhs = received[0:8, :]
    for z in range(1, N_Z):
        rhs = rhs + received[z * 8 : z * 8 + 8, :]
    solved = mm(rhs, rows[...], NT, precision=EXACT)
    for z in range(N_Z):
        out[z * 8 : z * 8 + 8, :] = solved


def give_back(received, pick, out):
    solved = jnp.concatenate([received[z * 8 : z * 8 + 8, :] for z in range(N_Z)], axis=1)
    three = mm(jnp.concatenate(pieces(solved, 3), axis=0), pick[...])
    every = three[0:8] + three[8:16] + three[16:24]
    groups = [every[:, g * 128 : (g + 1) * 128] for g in range(6)]
    for m in range(PEERS):
        base, keep, moves = layout(m)
        tile = jnp.where(lanes_in(keep), groups[base], 0.0)
        for here, group, there in moves:
            tile = jnp.where(lanes_in([here]), roll_slots(groups[group], here - there), tile)
        out[m * 8 : m * 8 + 8, :] = tile


def first_direction(
    schur, rows, columns, me, stiffness, solved, r, e0, e1, e2, e3, g0, g1, g2, g3,
    send, p_out, dots, q0, q1, q2, q3, wide,
):
    weights = slot_weights(me, stiffness)
    norm = jnp.zeros((1, NRHS), F32)
    curvature = jnp.zeros((1, NRHS), F32)
    total = jnp.zeros((128, NRHS), F32)
    for k, (e, g) in enumerate(zip((e0, e1, e2, e3), (g0, g1, g2, g3))):
        p = e[...] + g[...] + mm(columns[rows_of(k), :], solved[...], NT, precision=EXACT)
        p_out[rows_of(k), :] = p
        norm = norm + weights[k] * jnp.sum(r[rows_of(k), :] * p, axis=0, keepdims=True)
        split_into(wide, k, p)
    for k, q in enumerate((q0, q1, q2, q3)):
        value = block_product(schur, wide, k)
        q[...] = value
        curvature = curvature + jnp.sum(value * p_out[rows_of(k), :], axis=0, keepdims=True)
        total = total + mm(rows[:, rows_of(k)], value, precision=EXACT)
    send[...] = jnp.transpose(total)
    dots[0:1, :] = norm
    dots[1:2, :] = curvature


def second_local(
    inverse, me, stiffness, q0, q1, q2, q3, g0, g1, g2, g3, t_out, e0, e1, e2, e3, wide
):
    weights = slot_weights(me, stiffness)
    for k, (q, g) in enumerate(zip((q0, q1, q2, q3), (g0, g1, g2, g3))):
        t = q[...] + g[...]
        t_out[rows_of(k), :] = t
        split_into(wide, k, weights[k] * t)
    for k, e in enumerate((e0, e1, e2, e3)):
        e[...] = weights[k] * block_product(inverse, wide, k)


def second_direction(
    schur, columns, me, stiffness, solved, dots, t, e0, e1, e2, e3, g0, g1, g2, g3,
    send, v_out, u0, u1, u2, u3, wide,
):
    weights = slot_weights(me, stiffness)
    first = jnp.zeros((1, NRHS), F32)
    second = jnp.zeros((1, NRHS), F32)
    for k, (e, g) in enumerate(zip((e0, e1, e2, e3), (g0, g1, g2, g3))):
        v = e[...] + g[...] + mm(columns[rows_of(k), :], solved[...], NT, precision=EXACT)
        v_out[rows_of(k), :] = v
        first = first + weights[k] * jnp.sum(t[rows_of(k), :] * v, axis=0, keepdims=True)
        split_into(wide, k, v)
    for k, u in enumerate((u0, u1, u2, u3)):
        value = block_product(schur, wide, k)
        u[...] = value
        second = second + jnp.sum(value * v_out[rows_of(k), :], axis=0, keepdims=True)
    values = (dots[0:1, :], dots[1:2, :], first, second)
    tile = jnp.concatenate([v[:, :128] for v in values] + [v[:, 128:] for v in values], axis=0)
    for m in range(PEERS):
        send[m * 8 : m * 8 + 8, :] = tile


def add_plane(received, out):
    total = received[0:8, :]
    for m in range(1, PEERS):
        total = total + received[m * 8 : m * 8 + 8, :]
    for z in range(N_Z):
        out[z * 8 : z * 8 + 8, :] = total


def finish(
    received, dof, r, p, t, v, u0, u1, u2, u3, g0, g1, g2, g3, x_out, r_out, perm_t, wide
):
    total = received[0:8, :]
    for z in range(1, N_Z):
        total = total + received[z * 8 : z * 8 + 8, :]
    norm, curvature, g, h = (
        jnp.concatenate([total[i : i + 1], total[i + 4 : i + 5]], axis=1) for i in range(4)
    )
    step = norm / curvature
    scaled = step * g
    grown = scaled / curvature
    next_norm = (grown - 1.0) * norm
    next_curvature = step * (step * h) - grown * scaled
    next_step = next_norm / next_curvature
    for k, (u, halo) in enumerate(zip((u0, u1, u2, u3), (g0, g1, g2, g3))):
        rows = rows_of(k)
        w = u[...] + halo[...]
        both = step + next_step * grown
        solution = both * p[rows, :] - (next_step * step) * v[rows, :]
        residual = r[rows, :] - both * t[rows, :] + (next_step * step) * w
        for i, part in enumerate(pieces(solution, 3)):
            wide[rows, i * NRHS : (i + 1) * NRHS] = part
        for i, part in enumerate(pieces(residual, 3)):
            wide[rows, (i + 3) * NRHS : (i + 4) * NRHS] = part
    for k, block in enumerate(unknown_major(dof[...])):
        perm_t[:, rows_of(k)] = block
    for k in range(4):
        rows = rows_of(k)
        for j, out in enumerate((x_out, r_out)):
            three = mm(perm_t[rows, :], wide[:, 3 * j * NRHS : 3 * (j + 1) * NRHS])
            out[rows, :] = three[:, :NRHS] + three[:, NRHS : 2 * NRHS] + three[:, 2 * NRHS :]


PLANES = [[s * N_DEV + z * N_X + x for s in range(N_SUB) for x in range(N_X)] for z in range(N_Z)]
LINES = [[z * N_X + x for z in range(N_Z)] for x in range(N_X)]


def over_plane(v):
    return lax.all_to_all(v, ("sub", "dev"), 0, 0, tiled=True, axis_index_groups=PLANES)


def over_line(v):
    return lax.all_to_all(v, "dev", 0, 0, tiled=True, axis_index_groups=LINES)


def ring(v, axis, count, shift):
    return lax.ppermute(v, axis, [(i, (i + shift) % count) for i in range(count)])


def halo(blocks):
    return [
        ring(blocks[1], "sub", N_SUB, 1),
        ring(blocks[0], "sub", N_SUB, -1),
        ring(blocks[3], "dev", N_DEV, 1),
        ring(blocks[2], "dev", N_DEV, -1),
    ]


def shards(
    load, schur, local_inverse, coarse_basis, coarse_inverse, dof_lists, coarse_map, stiffness
):
    me = jnp.stack([lax.axis_index("sub"), lax.axis_index("dev")]).astype(jnp.int32)
    dof = dof_lists[0]
    names = jnp.broadcast_to(jnp.tile(coarse_map, (1, 8)).astype(F32), (8, 128))
    block = shape(CAP, NRHS)
    vector = shape(NI, NRHS)
    square = shape(NI, NI, dtype=BF16)
    wide = pltpu.VMEM((NI, 2 * NRHS), BF16)
    big = 2 * NI * NI * NRHS

    hs = run(
        prepare,
        [shape(HROWS, NRHS)] * 4,
        [me, stiffness, dof, load, coarse_basis, names],
        smem=(0, 1),
        scratch=[pltpu.VMEM((NI, 3 * NRHS), BF16), pltpu.VMEM((NI, NI), BF16)],
        flops=3 * big,
    )
    gs = halo(hs)
    planes = [coarse_inverse] + [
        lax.ppermute(
            coarse_inverse,
            "dev",
            [(z * N_X + x, z * N_X + (x + i) % N_X) for z in range(N_Z) for x in range(N_X)],
        )
        for i in range(1, N_X)
    ]
    schur_s, inverse_s = run(
        permute_blocks,
        [square, square],
        [dof, schur, local_inverse],
        scratch=[pltpu.VMEM((NI, NI), BF16)] * 3,
        flops=16 * big,
    )
    send, rows, columns, r, *es = run(
        begin,
        [shape(PEERS * 16, 128), shape(128, NI), shape(NI, 128), vector] + [block] * 4,
        [me, stiffness, inverse_s, *hs, *gs],
        smem=(0, 1),
        scratch=[wide],
        flops=2 * big,
    )
    es_halo = halo(es)
    line, pick = run(
        gather_first,
        [shape(N_Z * 8, NC), shape(NC, 768, dtype=BF16)],
        [over_plane(send)],
    )

    def coarse_tail(line):
        (part,) = run(
            coarse_solve,
            [shape(N_Z * 8, 128)],
            [me, over_line(line), *planes],
            smem=(0,),
            scratch=[pltpu.VMEM((128, NC), F32)],
        )
        (back,) = run(give_back, [shape(PEERS * 8, 128)], [over_line(part), pick])
        return over_plane(back)

    solved = coarse_tail(line)
    send, p, dots, *qs = run(
        first_direction,
        [shape(PEERS * 8, 128), vector, shape(8, NRHS)] + [block] * 4,
        [schur_s, rows, columns, me, stiffness, solved, r, *es, *es_halo],
        smem=(3, 4),
        scratch=[wide],
        flops=2 * big,
    )
    qs_halo = halo(qs)
    (line,) = run(gather_again, [shape(N_Z * 8, NC)], [over_plane(send), pick])
    t, *es = run(
        second_local,
        [vector] + [block] * 4,
        [inverse_s, me, stiffness, *qs, *qs_halo],
        smem=(1, 2),
        scratch=[wide],
        flops=2 * big,
    )
    es_halo = halo(es)
    solved = coarse_tail(line)
    send, v, *us = run(
        second_direction,
        [shape(PEERS * 8, 128), vector] + [block] * 4,
        [schur_s, columns, me, stiffness, solved, dots, t, *es, *es_halo],
        smem=(2, 3),
        scratch=[wide],
        flops=2 * big,
    )
    us_halo = halo(us)
    (line,) = run(add_plane, [shape(N_Z * 8, 128)], [over_plane(send)])
    return tuple(
        run(
            finish,
            [vector, vector],
            [over_line(line), dof, r, p, t, v, *us, *us_halo],
            scratch=[pltpu.VMEM((NI, NI), BF16), pltpu.VMEM((NI, 6 * NRHS), BF16)],
            flops=6 * big,
        )
    )


def solution(mesh):
    placed = (
        P(("sub", "dev"), None),
        P(("sub", "dev"), None),
        P(("sub", "dev"), None),
        P(("sub", "dev"), None),
        P("dev", None),
        P(("sub", "dev"), None, None),
        P(("sub", "dev"), None),
        P(),
    )
    return jax.shard_map(
        shards,
        mesh=mesh,
        in_specs=placed,
        out_specs=(P(("sub", "dev"), None), P(("sub", "dev"), None)),
        check_vma=False,
    )
```

time: 1140 us -> 228 us (0.20)
  waiting for transfers between devices: 666 us -> 29.1 us
  blocking collectives: 236 us -> 73.8 us
  other arithmetic: 76.2 us -> 0.73 us
  Pallas kernels: 0 us -> 37.3 us
  matrix products: 26.6 us -> 0 us
  local copies, waits for them, and re-layouts: 50.8 us -> 30 us
  between operations: 14.4 us -> 1 us
    psum x2 -> x0, waiting for transfers between devices: 508 us -> none  [coarse_sum(): return lax.psum(coarse_term(weighted_vector), ('sub', 'dev'))]
    psum x3 -> x0, blocking collectives: 236 us -> none  [global_dot(): return lax.psum(jnp.sum(weights * left * right, axis=0), ('sub', 'dev'))]
    all_gather x2 -> x0, waiting for transfers between devices: 141 us -> none  [precondition(): solved = lax.all_gather(solved_rows, 'dev', axis=0, tiled=True)]
    all_to_all x0 -> x6, blocking collectives: none -> 73.8 us  [the longest x3 40.4 us: over_plane(): lax.all_to_all(v, ('sub', 'dev'), 0, 0, tiled=True, axis_index_groups=PLA...]
    scatter-add x5 -> x0, other arithmetic: 46.9 us -> none  [assemble(): padded.at[target.reshape(-1)].add(incoming.reshape(-1, values.shape[1]))]
    pallas_call x0 -> x14, Pallas kernels: none -> 37.3 us  [run(): pl.pallas_call(body, out_shape=list(outs), in_specs=specs, out_specs=[vme...]
    ppermute x20 -> x23, starting transfers between devices: 65.4 us -> 29.8 us  [the longest x20 27.7 us: ring(): lax.ppermute(v, axis, [(i, (i + shift) % count) for i in range(count)])]
    gather x6 -> x0, local copies, waits for them, and re-layouts: 27.7 us -> none  [the longest x5 27.1 us: assemble(): packed = values[safe_rows] * in_use_float]
  transfers between devices with their start and end apart: 24 -> 27, of which waited for: 15 -> 8; matrix products, arithmetic and copies ran while one was open for 1% -> 0% of each run, Pallas kernels for 0% -> 7%
where the time goes in v1:
time: 228 us; the launch traced here: 226 us
  blocking collectives  73.8 us (32%)
  starting transfers between devices  54.6 us (24%)
  Pallas kernels  37.3 us (16%)
  local copies, waits for them, and re-layouts  30 us (13%)
  waiting for transfers between devices  29.1 us (13%)
    all_to_all x3, blocking collectives, over_plane(): lax.all_to_all(v, ('sub', 'dev'), 0, 0, tiled=True, axis_index_groups=PLA...  40.4 us
    pallas_call x14, Pallas kernels, run(): pl.pallas_call(body, out_shape=list(outs), in_specs=specs, out_specs=[vme...  37.3 us
    all_to_all x3, blocking collectives, over_line(): return lax.all_to_all(v, 'dev', 0, 0, tiled=True, axis_index_groups=LINES)  33.4 us
    unnamed x92, local copies, waits for them, and re-layouts  29.9 us
    ppermute x20, starting transfers between devices, ring(): lax.ppermute(v, axis, [(i, (i + shift) % count) for i in range(count)])  27.7 us
    all_to_all x2, starting transfers between devices, over_plane(): lax.all_to_all(v, ('sub', 'dev'), 0, 0, tiled=True, axis_index_groups=PLA...  15.9 us
    all_to_all x2, waiting for transfers between devices, over_plane(): lax.all_to_all(v, ('sub', 'dev'), 0, 0, tiled=True, axis_index_groups=PLA...  15.2 us
    ppermute x20, waiting for transfers between devices, ring(): lax.ppermute(v, axis, [(i, (i + shift) % count) for i in range(count)])  11.8 us
  transfers between devices with their start and end apart: 27, of which 8 were waited for; matrix products, arithmetic and copies ran while one was open for 0% of the time, Pallas kernels for 7%

profile of v1, /device:TPU:1, one launch (start us, length us, event | category | flops | bytes accessed | tf_op | source)
XLA Modules:
  0.0 226.5 jit_solution(16862046025738373723)
XLA Ops:
  2.1 1.2 copy-done.40
  4.9 3.1 %prepare.1 = (f32[280,256]{1,0:T(8,128)S(1)}, f32[280,256]{1,0:T(8,128)S(1)}, f32[280,256]{1,0:T(8,128)S(1)}, f32[280,256]{1,0:T(8,128)S(1)}) custom-call(s32[2]{0:T(128)S(1)} %pad_add_fusion.me, f32[256]{0:T(256)S(1)} %copy-done.36, s32[4,256]{1,0:T(4,128)S(1)} %bitcast.42, f32[1024,256]{1,0:T(8,128)S(1)} %copy-done.40, f32[16,1024]{1,0:T(8,128)S(1)} %copy-done.43, ...), custom_call_target="tpu_custom_call" | custom-call | flops 1610612736 | bytes 2270216 | tf_op jit(solution)/shard_map/prepare/pallas_call | solution.py:41
  8.0 3.3 %collective-permute-start.1 = (f32[280,256]{1,0:T(8,128)S(1)}, f32[280,256]{1,0:T(8,128)S(1)}, u32[]{:S(2)}, u32[]{:S(2)}) collective-permute-start(f32[280,256]{1,0:T(8,128)S(1)} %get-tuple-element.38.h0), channel_id=1, source_target_pairs={{0,224},{32,0},{64,32},{96,64},{128,96},{160,128},{192,160},{224,1... | collective-permute-start | bytes 860168 | tf_op jit(solution)/shard_map/ppermute | solution.py:383
  11.3 7.2 %collective-permute-start.3 = (f32[280,256]{1,0:T(8,128)S(1)}, f32[280,256]{1,0:T(8,128)S(1)}, u32[]{:S(2)}, u32[]{:S(2)}) collective-permute-start(f32[280,256]{1,0:T(8,128)S(1)} %get-tuple-element.40.h2), channel_id=1, source_target_pairs={{0,31},{1,0},{2,1},{3,2},{4,3},{5,4},{6,5},{7,6},{8,7},{9,8},{10,9... | collective-permute-start | bytes 860168 | tf_op jit(solution)/shard_map/ppermute | solution.py:383
  18.5 9.3 %permute_blocks.1 = (bf16[1024,1024]{1,0:T(8,128)(2,1)S(1)}, bf16[1024,1024]{1,0:T(8,128)(2,1)S(1)}) custom-call(s32[4,256]{1,0:T(4,128)S(1)} %bitcast.43, bf16[1024,1024]{1,0:T(8,128)(2,1)S(1)} %copy-done.38, bf16[1024,1024]{1,0:T(8,128)(2,1)S(1)} %copy-done.39), custom_call_target="tpu_custom_call" | custom-call | flops 8589934592 | bytes 8392704 | tf_op jit(solution)/shard_map/permute_blocks/pallas_call | solution.py:41
  27.8 1.3 copy-done.2
  29.1 2.5 %begin.1 = (f32[512,128]{1,0:T(8,128)S(1)}, f32[128,1024]{1,0:T(8,128)S(1)}, f32[1024,128]{1,0:T(8,128)S(1)}, f32[1024,256]{1,0:T(8,128)S(1)}, f32[256,256]{1,0:...) custom-call(s32[2]{0:T(128)S(1)} %pad_add_fusion.me, f32[256]{0:T(256)S(1)} %copy-done.37, ...), custom_call_target="tpu_custom_call" | custom-call | flops 1073741824 | bytes 7799816 | tf_op jit(solution)/shard_map/begin/pallas_call | solution.py:41
  35.3 15.1 %all_to_all.110 = f32[32,16,128]{2,1,0:T(8,128)S(1)} all-to-all(f32[32,16,128]{2,1,0:T(8,128)S(1)} %bitcast.33), channel_id=1, replica_groups={{0,1,2,3,32,33,34,35,64,65,66,67,96,97,98,99,128,129,130,131,160,161,16..., dimensions={0} | all-to-all | bytes 524288 | tf_op jit(solution)/shard_map/all_to_all | solution.py:375
  51.9 5.4 %all-to-all-start.1 = ((f32[8,8,1024]{2,1,0:T(8,128)}), f32[8,8,1024]{2,1,0:T(8,128)S(1)}, u32[]{:S(2)}, u32[]{:S(2)}) async-start(f32[8,8,1024]{2,1,0:T(8,128)} %bitcast.32), calls=%async_computation.1 | async-start | bytes 524288 | tf_op jit(solution)/shard_map/all_to_all | solution.py:379
  58.3 1.2 collective-permute-start.5
  59.5 1.2 collective-permute-start.8
  62.7 4.2 %collective-permute-start.10 = (f32[256,256]{1,0:T(8,128)}, f32[256,256]{1,0:T(8,128)}, u32[]{:S(2)}, u32[]{:S(2)}) collective-permute-start(f32[256,256]{1,0:T(8,128)} %copy-done.23), channel_id=1, source_target_pairs={{0,31},{1,0},{2,1},{3,2},{4,3},{5,4},{6,5},{7,6},{8,7},{9,8},{10,9... | collective-permute-start | bytes 786440 | tf_op jit(solution)/shard_map/ppermute | solution.py:383
  68.4 1.3 all-to-all-done.1
  72.3 1.1 coarse_solve.2
  73.4 11.7 %all_to_all.111 = f32[8,8,128]{2,1,0:T(8,128)S(1)} all-to-all(f32[8,8,128]{2,1,0:T(8,128)S(1)} %bitcast.37), channel_id=1, replica_groups={{0,4,8,12,16,20,24,28},{1,5,9,13,17,21,25,29},{2,6,10,14,18,22,26,30},{..., dimensions={0} | all-to-all | bytes 65536 | tf_op jit(solution)/shard_map/all_to_all | solution.py:379
  85.2 1.1 give_back.2
  86.3 9.0 %all-to-all-start.3 = ((f32[32,8,128]{2,1,0:T(8,128)}), f32[32,8,128]{2,1,0:T(8,128)S(1)}, u32[]{:S(2)}, u32[]{:S(2)}) async-start(f32[32,8,128]{2,1,0:T(8,128)} %bitcast.10), calls=%async_computation.3 | async-start | bytes 262144 | tf_op jit(solution)/shard_map/all_to_all | solution.py:375
  95.3 7.6 %all-to-all-done.3 = f32[32,8,128]{2,1,0:T(8,128)S(1)} async-done(((f32[32,8,128]{2,1,0:T(8,128)}), f32[32,8,128]{2,1,0:T(8,128)S(1)}, u32[]{:S(2)}, u32[]{:S(2)}) %all-to-all-start.3) | async-done | bytes 131104 | tf_op jit(solution)/shard_map/all_to_all | solution.py:375
  102.9 1.6 copy-done.3
  104.5 1.0 copy-done.18
  105.6 0.9 copy-done.20
  106.5 0.9 copy-done.22
  107.5 0.9 copy-done.24
  108.4 0.9 copy-done.26
  109.4 4.4 %first_direction.1 = (f32[256,128]{1,0:T(8,128)S(1)}, f32[1024,256]{1,0:T(8,128)S(1)}, f32[8,256]{1,0:T(8,128)S(1)}, f32[256,256]{1,0:T(8,128)S(1)}, f32[256,256...) custom-call(bf16[1024,1024]{1,0:T(8,128)(2,1)S(1)} %copy-done.3, f32[128,1024]{1,0:T(8,128)S(1)} %copy-done.18, ...), custom_call_target="tpu_custom_call" | custom-call | flops 1073741824 | bytes 8659976 | tf_op jit(solution)/shard_map/first_direction/pallas_call | solution.py:41
  113.8 11.5 %all_to_all.112 = f32[32,8,128]{2,1,0:T(8,128)S(1)} all-to-all(f32[32,8,128]{2,1,0:T(8,128)S(1)} %bitcast.40), channel_id=1, replica_groups={{0,1,2,3,32,33,34,35,64,65,66,67,96,97,98,99,128,129,130,131,160,161,16..., dimensions={0} | all-to-all | bytes 262144 | tf_op jit(solution)/shard_map/all_to_all | solution.py:375
  125.3 1.3 gather_again.1
  126.6 3.4 %all-to-all-start.5 = ((f32[8,8,1024]{2,1,0:T(8,128)}), f32[8,8,1024]{2,1,0:T(8,128)S(1)}, u32[]{:S(2)}, u32[]{:S(2)}) async-start(f32[8,8,1024]{2,1,0:T(8,128)} %bitcast.14), calls=%async_computation.5 | async-start | bytes 524288 | tf_op jit(solution)/shard_map/all_to_all | solution.py:379
  130.4 1.5 collective-permute-start.11
  131.8 3.0 %collective-permute-start.14 = (f32[256,256]{1,0:T(8,128)}, f32[256,256]{1,0:T(8,128)S(1)}, u32[]{:S(2)}, u32[]{:S(2)}) collective-permute-start(f32[256,256]{1,0:T(8,128)} %copy-done.31), channel_id=1, source_target_pairs={{0,31},{1,0},{2,1},{3,2},{4,3},{5,4},{6,5},{7,6},{8,7},{9,8},{10,9... | collective-permute-start | bytes 786440 | tf_op jit(solution)/shard_map/ppermute | solution.py:383
  134.8 1.5 collective-permute-done.12.g1
  136.4 6.2 %collective-permute-done.14.g3 = f32[256,256]{1,0:T(8,128)S(1)} collective-permute-done((f32[256,256]{1,0:T(8,128)}, f32[256,256]{1,0:T(8,128)S(1)}, u32[]{:S(2)}, u32[]{:S(2)}) %collective-permute-start.14) | collective-permute-done | bytes 262176 | tf_op jit(solution)/shard_map/ppermute | solution.py:383
  142.5 4.0 %collective-permute-done.13.g2 = f32[256,256]{1,0:T(8,128)S(1)} collective-permute-done((f32[256,256]{1,0:T(8,128)}, f32[256,256]{1,0:T(8,128)S(1)}, u32[]{:S(2)}, u32[]{:S(2)}) %collective-permute-start.13) | collective-permute-done | bytes 262176 | tf_op jit(solution)/shard_map/ppermute | solution.py:383
  146.6 1.6 copy-done.1
  149.1 0.9 copy-done.30
  152.0 2.6 %second_local.1 = (f32[1024,256]{1,0:T(8,128)S(1)}, f32[256,256]{1,0:T(8,128)}, f32[256,256]{1,0:T(8,128)}, f32[256,256]{1,0:T(8,128)}, f32[256,256]{1,0:T(8,128)}) custom-call(bf16[1024,1024]{1,0:T(8,128)(2,1)S(1)} %copy-done.1, s32[2]{0:T(128)S(1)} %pad_add_fusion.me, f32[256]{0:T(256)S(1)} %copy-done.37, f32[256,256]{1,0:T(8,128)S(1)} %copy-done.28, ...), custom_call_target="tpu_custom_call" | custom-call | flops 1073741824 | bytes 6292488 | tf_op jit(solution)/shard_map/second_local/pallas_call | solution.py:41
  156.4 1.4 collective-permute-start.18
  160.5 1.1 coarse_solve.3
  161.6 12.1 %all_to_all.113 = f32[8,8,128]{2,1,0:T(8,128)S(1)} all-to-all(f32[8,8,128]{2,1,0:T(8,128)S(1)} %bitcast.34), channel_id=1, replica_groups={{0,4,8,12,16,20,24,28},{1,5,9,13,17,21,25,29},{2,6,10,14,18,22,26,30},{..., dimensions={0} | all-to-all | bytes 65536 | tf_op jit(solution)/shard_map/all_to_all | solution.py:379
  173.8 1.1 give_back.3
  174.9 6.9 %all-to-all-start.7 = ((f32[32,8,128]{2,1,0:T(8,128)}), f32[32,8,128]{2,1,0:T(8,128)S(1)}, u32[]{:S(2)}, u32[]{:S(2)}) async-start(f32[32,8,128]{2,1,0:T(8,128)} %bitcast.18), calls=%async_computation.7 | async-start | bytes 262144 | tf_op jit(solution)/shard_map/all_to_all | solution.py:375
  181.8 7.6 %all-to-all-done.7 = f32[32,8,128]{2,1,0:T(8,128)S(1)} async-done(((f32[32,8,128]{2,1,0:T(8,128)}), f32[32,8,128]{2,1,0:T(8,128)S(1)}, u32[]{:S(2)}, u32[]{:S(2)}) %all-to-all-start.7) | async-done | bytes 131104 | tf_op jit(solution)/shard_map/all_to_all | solution.py:375
  189.4 1.6 copy-done.4
  191.0 3.8 %second_direction.1 = (f32[256,128]{1,0:T(8,128)S(1)}, f32[1024,256]{1,0:T(8,128)S(1)}, f32[256,256]{1,0:T(8,128)S(1)}, f32[256,256]{1,0:T(8,128)S(1)}, f32[256,256]{1,0:T(8,128)S(1)}, /*index=5*/f32[256,256]{1,0:T(8,128)S(1)}) custom-call(bf16[1024,1024]{1,0:T(8,128)(2,1)S(1)} %copy-done.4, f32[1024,128]{1,0:T(8,128)S(1)} %get-tuple-element.42.columns, ...), custom_call_target="tpu_custom_call" | custom-call | flops 1073741824 | bytes 8135688 | tf_op jit(solution)/shard_map/second_direction/pallas_call | solution.py:41
  195.1 1.5 collective-permute-start.19
  198.0 13.9 %all_to_all.114 = f32[32,8,128]{2,1,0:T(8,128)S(1)} all-to-all(f32[32,8,128]{2,1,0:T(8,128)S(1)} %bitcast.39), channel_id=1, replica_groups={{0,1,2,3,32,33,34,35,64,65,66,67,96,97,98,99,128,129,130,131,160,161,16..., dimensions={0} | all-to-all | bytes 262144 | tf_op jit(solution)/shard_map/all_to_all | solution.py:375
  211.9 9.5 %all_to_all.115 = f32[8,8,128]{2,1,0:T(8,128)S(1)} all-to-all(f32[8,8,128]{2,1,0:T(8,128)S(1)} %bitcast.38), channel_id=1, replica_groups={{0,4,8,12,16,20,24,28},{1,5,9,13,17,21,25,29},{2,6,10,14,18,22,26,30},{..., dimensions={0} | all-to-all | bytes 65536 | tf_op jit(solution)/shard_map/all_to_all | solution.py:379
  221.5 5.0 %finish.1 = (f32[1024,256]{1,0:T(8,128)}, f32[1024,256]{1,0:T(8,128)}) custom-call(f32[64,128]{1,0:T(8,128)S(1)} %bitcast.41, s32[4,256]{1,0:T(4,128)S(1)} %bitcast.44, f32[1024,256]{1,0:T(8,128)S(1)} %copy-done.6, f32[1024,256]{1,0:T(8,128)S(1)} %copy-done.42, f32[1024,256]{1,0:T(8,128)S(1)} %get-tuple-element.58.t, f32[1024,256]{1,0:T(8,128)S(1)} %get-tuple-element.65.v, ...), custom_call_target="tpu_custom_call" | custom-call | flops 3221225472 | bytes 8425472 | tf_op jit(solution)/shard_map/finish/pallas_call | solution.py:41
  (123 shorter events, 24.9 us)
Async XLA Ops:
  2.1 1.2 copy-start.40
  4.9 13.6 %copy-start.38 = (bf16[1024,1024]{1,0:T(8,128)(2,1)S(1)}, bf16[1024,1024]{1,0:T(8,128)(2,1)}, u32[]{:S(2)}) copy-start(bf16[1024,1024]{1,0:T(8,128)(2,1)} %schur.1) | copy-start | bytes 6291460
  4.9 13.6 %copy-start.39 = (bf16[1024,1024]{1,0:T(8,128)(2,1)S(1)}, bf16[1024,1024]{1,0:T(8,128)(2,1)}, u32[]{:S(2)}) copy-start(bf16[1024,1024]{1,0:T(8,128)(2,1)} %inverse.1) | copy-start | bytes 6291460
  8.0 21.1 %collective-permute-start.1 = (f32[280,256]{1,0:T(8,128)S(1)}, f32[280,256]{1,0:T(8,128)S(1)}, u32[]{:S(2)}, u32[]{:S(2)}) collective-permute-start(f32[280,256]{1,0:T(8,128)S(1)} %get-tuple-element.38.h0), channel_id=1, source_target_pairs={{0,224},{32,0},{64,32},{96,64},{128,96},{160,128},{192,160},{224,1... | collective-permute-start | bytes 860168 | tf_op jit(solution)/shard_map/ppermute | solution.py:383
  11.3 17.8 %collective-permute-start = (f32[280,256]{1,0:T(8,128)S(1)}, f32[280,256]{1,0:T(8,128)S(1)}, u32[]{:S(2)}, u32[]{:S(2)}) collective-permute-start(f32[280,256]{1,0:T(8,128)S(1)} %get-tuple-element.39.h1), channel_id=1, source_target_pairs={{0,32},{32,64},{64,96},{96,128},{128,160},{160,192},{192,224},{224... | collective-permute-start | bytes 860168 | tf_op jit(solution)/shard_map/ppermute | solution.py:383
  11.3 17.9 %collective-permute-start.3 = (f32[280,256]{1,0:T(8,128)S(1)}, f32[280,256]{1,0:T(8,128)S(1)}, u32[]{:S(2)}, u32[]{:S(2)}) collective-permute-start(f32[280,256]{1,0:T(8,128)S(1)} %get-tuple-element.40.h2), channel_id=1, source_target_pairs={{0,31},{1,0},{2,1},{3,2},{4,3},{5,4},{6,5},{7,6},{8,7},{9,8},{10,9... | collective-permute-start | bytes 860168 | tf_op jit(solution)/shard_map/ppermute | solution.py:383
  18.5 10.6 %copy-start.37 = (f32[256]{0:T(256)S(1)}, f32[256]{0:T(256)}, u32[]{:S(2)}) copy-start(f32[256]{0:T(256)} %stiffness.9) | copy-start | bytes 3076
  18.5 10.6 %collective-permute-start.2 = (f32[280,256]{1,0:T(8,128)S(1)}, f32[280,256]{1,0:T(8,128)S(1)}, u32[]{:S(2)}, u32[]{:S(2)}) collective-permute-start(f32[280,256]{1,0:T(8,128)S(1)} %get-tuple-element.41.h3), channel_id=1, source_target_pairs={{0,1},{1,2},{2,3},{3,4},{4,5},{5,6},{6,7},{7,8},{8,9},{9,10},{10,1... | collective-permute-start | bytes 860168 | tf_op jit(solution)/shard_map/ppermute | solution.py:383
  27.8 1.3 copy-start.2
  29.1 2.5 %copy-start = (bf16[1024,1024]{1,0:T(8,128)(2,1)}, bf16[1024,1024]{1,0:T(8,128)(2,1)S(1)}, u32[]{:S(2)}) copy-start(bf16[1024,1024]{1,0:T(8,128)(2,1)S(1)} %get-tuple-element.37.inverse) | copy-start | bytes 6291460
  29.1 28.2 %copy-start.7 = (f32[32,1024]{1,0:T(8,128)S(1)}, f32[32,1024]{1,0:T(8,128)}, u32[]{:S(2)}) copy-start(f32[32,1024]{1,0:T(8,128)} %k0.3) | copy-start | bytes 393220
  35.3 67.7 %copy-start.5 = (f32[1024,256]{1,0:T(8,128)}, f32[1024,256]{1,0:T(8,128)S(1)}, u32[]{:S(2)}) copy-start(f32[1024,256]{1,0:T(8,128)S(1)} %get-tuple-element.47.r) | copy-start | bytes 3145732
  51.9 17.7 %all-to-all-start.1 = ((f32[8,8,1024]{2,1,0:T(8,128)}), f32[8,8,1024]{2,1,0:T(8,128)S(1)}, u32[]{:S(2)}, u32[]{:S(2)}) async-start(f32[8,8,1024]{2,1,0:T(8,128)} %bitcast.32), calls=%async_computation.1 | async-start | bytes 524288 | tf_op jit(solution)/shard_map/all_to_all | solution.py:379
  57.3 4.7 %collective-permute-start.6 = (f32[32,1024]{1,0:T(8,128)S(1)}, f32[32,1024]{1,0:T(8,128)S(1)}, u32[]{:S(2)}, u32[]{:S(2)}) collective-permute-start(f32[32,1024]{1,0:T(8,128)S(1)} %copy-done.7), channel_id=1, source_target_pairs={{0,3},{1,0},{2,1},{3,2},{4,7},{5,4},{6,5},{7,6},{8,11},{9,8},{10,9... | collective-permute-start | bytes 393224 | tf_op jit(solution)/shard_map/ppermute | solution.py:417
  58.3 8.6 %collective-permute-start.5 = (f32[32,1024]{1,0:T(8,128)S(1)}, f32[32,1024]{1,0:T(8,128)S(1)}, u32[]{:S(2)}, u32[]{:S(2)}) collective-permute-start(f32[32,1024]{1,0:T(8,128)S(1)} %copy-done.7), channel_id=1, source_target_pairs={{0,2},{1,3},{2,0},{3,1},{4,6},{5,7},{6,4},{7,5},{8,10},{9,11},{10,... | collective-permute-start | bytes 393224 | tf_op jit(solution)/shard_map/ppermute | solution.py:417
  59.5 8.2 %collective-permute-start.4 = (f32[32,1024]{1,0:T(8,128)S(1)}, f32[32,1024]{1,0:T(8,128)S(1)}, u32[]{:S(2)}, u32[]{:S(2)}) collective-permute-start(f32[32,1024]{1,0:T(8,128)S(1)} %copy-done.7), channel_id=1, source_target_pairs={{0,1},{1,2},{2,3},{3,0},{4,5},{5,6},{6,7},{7,4},{8,9},{9,10},{10,1... | collective-permute-start | bytes 393224 | tf_op jit(solution)/shard_map/ppermute | solution.py:417
  59.5 35.8 %collective-permute-start.8 = (f32[256,256]{1,0:T(8,128)}, f32[256,256]{1,0:T(8,128)}, u32[]{:S(2)}, u32[]{:S(2)}) collective-permute-start(f32[256,256]{1,0:T(8,128)} %copy-done.19), channel_id=1, source_target_pairs={{0,224},{32,0},{64,32},{96,64},{128,96},{160,128},{192,160},{224,1... | collective-permute-start | bytes 786440 | tf_op jit(solution)/shard_map/ppermute | solution.py:383
  60.7 34.6 %collective-permute-start.7 = (f32[256,256]{1,0:T(8,128)}, f32[256,256]{1,0:T(8,128)}, u32[]{:S(2)}, u32[]{:S(2)}) collective-permute-start(f32[256,256]{1,0:T(8,128)} %copy-done.21), channel_id=1, source_target_pairs={{0,32},{32,64},{64,96},{96,128},{128,160},{160,192},{192,224},{224... | collective-permute-start | bytes 786440 | tf_op jit(solution)/shard_map/ppermute | solution.py:383
  62.7 32.6 %collective-permute-start.10 = (f32[256,256]{1,0:T(8,128)}, f32[256,256]{1,0:T(8,128)}, u32[]{:S(2)}, u32[]{:S(2)}) collective-permute-start(f32[256,256]{1,0:T(8,128)} %copy-done.23), channel_id=1, source_target_pairs={{0,31},{1,0},{2,1},{3,2},{4,3},{5,4},{6,5},{7,6},{8,7},{9,8},{10,9... | collective-permute-start | bytes 786440 | tf_op jit(solution)/shard_map/ppermute | solution.py:383
  67.5 27.8 %collective-permute-start.9 = (f32[256,256]{1,0:T(8,128)}, f32[256,256]{1,0:T(8,128)}, u32[]{:S(2)}, u32[]{:S(2)}) collective-permute-start(f32[256,256]{1,0:T(8,128)} %copy-done.25), channel_id=1, source_target_pairs={{0,1},{1,2},{2,3},{3,4},{4,5},{5,6},{6,7},{7,8},{8,9},{9,10},{10,1... | collective-permute-start | bytes 786440 | tf_op jit(solution)/shard_map/ppermute | solution.py:383
  86.3 16.6 %all-to-all-start.3 = ((f32[32,8,128]{2,1,0:T(8,128)}), f32[32,8,128]{2,1,0:T(8,128)S(1)}, u32[]{:S(2)}, u32[]{:S(2)}) async-start(f32[32,8,128]{2,1,0:T(8,128)} %bitcast.10), calls=%async_computation.3 | async-start | bytes 262144 | tf_op jit(solution)/shard_map/all_to_all | solution.py:375
  102.9 1.6 copy-start.3
  104.5 1.0 copy-start.18
  105.6 0.9 copy-start.20
  113.8 12.8 %copy-start.27 = (f32[256,256]{1,0:T(8,128)}, f32[256,256]{1,0:T(8,128)S(1)}, u32[]{:S(2)}) copy-start(f32[256,256]{1,0:T(8,128)S(1)} %get-tuple-element.54.q0) | copy-start | bytes 786436
  113.8 12.8 %copy-start.29 = (f32[256,256]{1,0:T(8,128)}, f32[256,256]{1,0:T(8,128)S(1)}, u32[]{:S(2)}) copy-start(f32[256,256]{1,0:T(8,128)S(1)} %get-tuple-element.55.q1) | copy-start | bytes 786436
  113.8 12.8 %copy-start.31 = (f32[256,256]{1,0:T(8,128)}, f32[256,256]{1,0:T(8,128)S(1)}, u32[]{:S(2)}) copy-start(f32[256,256]{1,0:T(8,128)S(1)} %get-tuple-element.56.q2) | copy-start | bytes 786436
  113.8 12.8 %copy-start.33 = (f32[256,256]{1,0:T(8,128)}, f32[256,256]{1,0:T(8,128)S(1)}, u32[]{:S(2)}) copy-start(f32[256,256]{1,0:T(8,128)S(1)} %get-tuple-element.57.q3) | copy-start | bytes 786436
  113.8 12.8 %copy-start.41 = (f32[1024,256]{1,0:T(8,128)}, f32[1024,256]{1,0:T(8,128)S(1)}, u32[]{:S(2)}) copy-start(f32[1024,256]{1,0:T(8,128)S(1)} %get-tuple-element.64.p) | copy-start | bytes 3145732
  126.6 31.2 %all-to-all-start.5 = ((f32[8,8,1024]{2,1,0:T(8,128)}), f32[8,8,1024]{2,1,0:T(8,128)S(1)}, u32[]{:S(2)}, u32[]{:S(2)}) async-start(f32[8,8,1024]{2,1,0:T(8,128)} %bitcast.14), calls=%async_computation.5 | async-start | bytes 524288 | tf_op jit(solution)/shard_map/all_to_all | solution.py:379
  130.1 6.3 %collective-permute-start.12 = (f32[256,256]{1,0:T(8,128)}, f32[256,256]{1,0:T(8,128)S(1)}, u32[]{:S(2)}, u32[]{:S(2)}) collective-permute-start(f32[256,256]{1,0:T(8,128)} %copy-done.27), channel_id=1, source_target_pairs={{0,224},{32,0},{64,32},{96,64},{128,96},{160,128},{192,160},{224,1... | collective-permute-start | bytes 786440 | tf_op jit(solution)/shard_map/ppermute | solution.py:383
  130.4 6.0 %collective-permute-start.11 = (f32[256,256]{1,0:T(8,128)}, f32[256,256]{1,0:T(8,128)S(1)}, u32[]{:S(2)}, u32[]{:S(2)}) collective-permute-start(f32[256,256]{1,0:T(8,128)} %copy-done.29), channel_id=1, source_target_pairs={{0,32},{32,64},{64,96},{96,128},{128,160},{160,192},{192,224},{224... | collective-permute-start | bytes 786440 | tf_op jit(solution)/shard_map/ppermute | solution.py:383
  131.8 10.7 %collective-permute-start.14 = (f32[256,256]{1,0:T(8,128)}, f32[256,256]{1,0:T(8,128)S(1)}, u32[]{:S(2)}, u32[]{:S(2)}) collective-permute-start(f32[256,256]{1,0:T(8,128)} %copy-done.31), channel_id=1, source_target_pairs={{0,31},{1,0},{2,1},{3,2},{4,3},{5,4},{6,5},{7,6},{8,7},{9,8},{10,9... | collective-permute-start | bytes 786440 | tf_op jit(solution)/shard_map/ppermute | solution.py:383
  134.8 11.7 %collective-permute-start.13 = (f32[256,256]{1,0:T(8,128)}, f32[256,256]{1,0:T(8,128)S(1)}, u32[]{:S(2)}, u32[]{:S(2)}) collective-permute-start(f32[256,256]{1,0:T(8,128)} %copy-done.33), channel_id=1, source_target_pairs={{0,1},{1,2},{2,3},{3,4},{4,5},{5,6},{6,7},{7,8},{8,9},{9,10},{10,1... | collective-permute-start | bytes 786440 | tf_op jit(solution)/shard_map/ppermute | solution.py:383
  146.6 1.6 copy-start.1
  154.6 27.2 %collective-permute-start.16 = (f32[256,256]{1,0:T(8,128)}, f32[256,256]{1,0:T(8,128)}, u32[]{:S(2)}, u32[]{:S(2)}) collective-permute-start(f32[256,256]{1,0:T(8,128)} %get-tuple-element.59.e0), channel_id=1, source_target_pairs={{0,224},{32,0},{64,32},{96,64},{128,96},{160,128},{192,160},{224,1... | collective-permute-start | bytes 786440 | tf_op jit(solution)/shard_map/ppermute | solution.py:383
  155.5 26.3 %collective-permute-start.15 = (f32[256,256]{1,0:T(8,128)}, f32[256,256]{1,0:T(8,128)}, u32[]{:S(2)}, u32[]{:S(2)}) collective-permute-start(f32[256,256]{1,0:T(8,128)} %get-tuple-element.60.e1), channel_id=1, source_target_pairs={{0,32},{32,64},{64,96},{96,128},{128,160},{160,192},{192,224},{224... | collective-permute-start | bytes 786440 | tf_op jit(solution)/shard_map/ppermute | solution.py:383
  156.4 25.5 %collective-permute-start.18 = (f32[256,256]{1,0:T(8,128)}, f32[256,256]{1,0:T(8,128)}, u32[]{:S(2)}, u32[]{:S(2)}) collective-permute-start(f32[256,256]{1,0:T(8,128)} %get-tuple-element.61.e2), channel_id=1, source_target_pairs={{0,31},{1,0},{2,1},{3,2},{4,3},{5,4},{6,5},{7,6},{8,7},{9,8},{10,9... | collective-permute-start | bytes 786440 | tf_op jit(solution)/shard_map/ppermute | solution.py:383
  157.7 24.1 %collective-permute-start.17 = (f32[256,256]{1,0:T(8,128)}, f32[256,256]{1,0:T(8,128)}, u32[]{:S(2)}, u32[]{:S(2)}) collective-permute-start(f32[256,256]{1,0:T(8,128)} %get-tuple-element.62.e3), channel_id=1, source_target_pairs={{0,1},{1,2},{2,3},{3,4},{4,5},{5,6},{6,7},{7,8},{8,9},{9,10},{10,1... | collective-permute-start | bytes 786440 | tf_op jit(solution)/shard_map/ppermute | solution.py:383
  174.9 14.5 %all-to-all-start.7 = ((f32[32,8,128]{2,1,0:T(8,128)}), f32[32,8,128]{2,1,0:T(8,128)S(1)}, u32[]{:S(2)}, u32[]{:S(2)}) async-start(f32[32,8,128]{2,1,0:T(8,128)} %bitcast.18), calls=%async_computation.7 | async-start | bytes 262144 | tf_op jit(solution)/shard_map/all_to_all | solution.py:375
  189.4 1.6 copy-start.4
  191.0 30.5 %copy-start.6 = (f32[1024,256]{1,0:T(8,128)S(1)}, f32[1024,256]{1,0:T(8,128)}, u32[]{:S(2)}) copy-start(f32[1024,256]{1,0:T(8,128)} %copy-done.5) | copy-start | bytes 3145732
  191.0 30.5 %copy-start.42 = (f32[1024,256]{1,0:T(8,128)S(1)}, f32[1024,256]{1,0:T(8,128)}, u32[]{:S(2)}) copy-start(f32[1024,256]{1,0:T(8,128)} %copy-done.41) | copy-start | bytes 3145732
  191.0 30.5 %copy-start.45 = (s32[1,4,256]{2,1,0:T(4,128)S(1)}, s32[1,4,256]{2,1,0:T(4,128)}, u32[]{:S(2)}) copy-start(s32[1,4,256]{2,1,0:T(4,128)} %param.13) | copy-start | bytes 12292
  194.8 26.6 %collective-permute-start.20 = (f32[256,256]{1,0:T(8,128)S(1)}, f32[256,256]{1,0:T(8,128)S(1)}, u32[]{:S(2)}, u32[]{:S(2)}) collective-permute-start(f32[256,256]{1,0:T(8,128)S(1)} %get-tuple-element.66.u0), channel_id=1, source_target_pairs={{0,224},{32,0},{64,32},{96,64},{128,96},{160,128},{192,160},{224,1... | collective-permute-start | bytes 786440 | tf_op jit(solution)/shard_map/ppermute | solution.py:383
  195.1 26.3 %collective-permute-start.19 = (f32[256,256]{1,0:T(8,128)S(1)}, f32[256,256]{1,0:T(8,128)S(1)}, u32[]{:S(2)}, u32[]{:S(2)}) collective-permute-start(f32[256,256]{1,0:T(8,128)S(1)} %get-tuple-element.67.u1), channel_id=1, source_target_pairs={{0,32},{32,64},{64,96},{96,128},{128,160},{160,192},{192,224},{224... | collective-permute-start | bytes 786440 | tf_op jit(solution)/shard_map/ppermute | solution.py:383
  196.6 24.9 %collective-permute-start.22 = (f32[256,256]{1,0:T(8,128)S(1)}, f32[256,256]{1,0:T(8,128)S(1)}, u32[]{:S(2)}, u32[]{:S(2)}) collective-permute-start(f32[256,256]{1,0:T(8,128)S(1)} %get-tuple-element.68.u2), channel_id=1, source_target_pairs={{0,31},{1,0},{2,1},{3,2},{4,3},{5,4},{6,5},{7,6},{8,7},{9,8},{10,9... | collective-permute-start | bytes 786440 | tf_op jit(solution)/shard_map/ppermute | solution.py:383
  197.1 24.4 %collective-permute-start.21 = (f32[256,256]{1,0:T(8,128)S(1)}, f32[256,256]{1,0:T(8,128)S(1)}, u32[]{:S(2)}, u32[]{:S(2)}) collective-permute-start(f32[256,256]{1,0:T(8,128)S(1)} %get-tuple-element.69.u3), channel_id=1, source_target_pairs={{0,1},{1,2},{2,3},{3,4},{4,5},{5,6},{6,7},{7,8},{8,9},{9,10},{10,1... | collective-permute-start | bytes 786440 | tf_op jit(solution)/shard_map/ppermute | solution.py:383
  (25 other events, 20.6 us)
